TPU v7x, 32 devices: a whole 2x2x4 slice. The times are simulated.
32 devices in a mesh: row: 16 (over z, y, core), col: 2 (over x).
Axes of the slice: x: 2, y: 2, z: 4, core: 2. Of those that a mesh axis runs over, the one named last changes fastest.
Arguments:
- tail_factor: bfloat16 [2, 16384, 768], P(None, 'row', 'col'), may hold values from -0.03125 to 0.03125
- tail_solution: bfloat16 [2, 16384, 512], P(None, 'row', 'col'), may hold values from -6 to 6
- coupling: bfloat16 [3, 2, 256, 768], P(None, None, 'row'), may hold values from -0.25 to 0.25
- inverse_blocks: float32 [3, 2, 256, 256], P(None, None, 'row'), may hold values from -0.25 to 1.25
- sources: float32 [3, 2, 256, 512], P(None, None, 'row'), may hold values from -6 to 6
- station_map: int32 [512], P('col'), may hold values from 0 to 511
Outputs:
- solution: float32 [3, 2, 256, 512], P(None, None, 'row', 'col')
All inputs are finite; a program needn't handle non-finite values.
Results may differ from a plain program's by a relative error of at most 0.0027.
Values may be sent and summed in bfloat16 or wider, within the bound.
A program may use at most 64 MiB of HBM per device.

v0:
```python
import jax
import jax.numpy as jnp
from jax import lax
from jax.sharding import PartitionSpec as P


def conj_tproduct(factor_part, solution_part):
    real_part = jnp.einsum(
        "pq,pr->qr", factor_part[0], solution_part[0], preferred_element_type=jnp.float32
    ) + jnp.einsum(
        "pq,pr->qr", factor_part[1], solution_part[1], preferred_element_type=jnp.float32
    )
    imag_part = jnp.einsum(
        "pq,pr->qr", factor_part[0], solution_part[1], preferred_element_type=jnp.float32
    ) - jnp.einsum(
        "pq,pr->qr", factor_part[1], solution_part[0], preferred_element_type=jnp.float32
    )
    return jnp.stack([real_part, imag_part])


def complex_product(matrix, vectors):
    high = lax.Precision.HIGHEST
    real_part = jnp.dot(matrix[0], vectors[0], precision=high) - jnp.dot(
        matrix[1], vectors[1], precision=high
    )
    imag_part = jnp.dot(matrix[0], vectors[1], precision=high) + jnp.dot(
        matrix[1], vectors[0], precision=high
    )
    return jnp.stack([real_part, imag_part])


def shards(tail_factor, tail_solution, coupling, inverse_blocks, sources, station_map):
    panel_count = coupling.shape[0]
    panel_width = inverse_blocks.shape[3]
    local_rows = inverse_blocks.shape[2]
    rhs_local = tail_solution.shape[2]
    source_count = sources.shape[3]
    selector = (
        lax.broadcasted_iota(jnp.int32, (source_count, rhs_local), 0) == station_map[None, :]
    ).astype(jnp.float32)
    adjoint_rhs = jnp.einsum("kcps,sr->kcpr", sources, selector, precision=lax.Precision.HIGHEST)
    partial_value = conj_tproduct(
        lax.all_gather(tail_factor, "col", axis=2, tiled=True), tail_solution
    )
    partial_value = partial_value.reshape(2, panel_count, panel_width, rhs_local)
    solved = [None] * panel_count
    rounded = [None] * panel_count
    row_offset = lax.axis_index("row") * local_rows
    own_rhs = jnp.transpose(adjoint_rhs, (1, 0, 2, 3))
    placed_all = lax.dynamic_update_slice_in_dim(
        jnp.zeros_like(partial_value), own_rhs, row_offset, 2
    )
    base_rhs = lax.psum(placed_all - partial_value, "row")
    whole_coupling = lax.all_gather(coupling, "row", axis=2, tiled=True)
    gathered = [None] * panel_count
    for panel_index in range(panel_count - 1, -1, -1):
        full_y = base_rhs[:, panel_index]
        for later_panel in range(panel_index + 1, panel_count):
            block_cols = whole_coupling[later_panel][
                :, :, panel_index * panel_width : (panel_index + 1) * panel_width
            ]
            full_y = full_y - conj_tproduct(block_cols, gathered[later_panel])
        solved[panel_index] = complex_product(inverse_blocks[panel_index], full_y)
        rounded[panel_index] = solved[panel_index].astype(jnp.bfloat16)
        if panel_index > 0:
            gathered[panel_index] = lax.all_gather(rounded[panel_index], "row", axis=1, tiled=True)
    return jnp.stack(solved)


def solution(mesh):
    placed = (
        P(None, "row", "col"),
        P(None, "row", "col"),
        P(None, None, "row", None),
        P(None, None, "row", None),
        P(None, None, "row", None),
        P("col"),
    )
    return jax.shard_map(
        shards, mesh=mesh, in_specs=placed, out_specs=P(None, None, "row", "col"), check_vma=False
    )
```

profile of v0, /device:TPU:0, one launch (start us, length us, event | category | flops | bytes accessed | tf_op | source)
XLA Modules:
  0.0 241.3 jit_solution(13952889367215881411)
XLA Ops:
  6.5 0.7 all-gather.3.cloned.1.call-update
  7.5 0.3 convolution_bitcast_fusion
  8.2 3.4 %dynamic_update_slice.3 = f32[2,3,256,256]{2,3,0,1:T(8,128)S(1)} dynamic-update-slice(f32[2,3,256,256]{2,3,0,1:T(8,128)S(1)} %broadcast_in_dim.4, f32[2,3,16,256]{2,3,0,1:T(8,128)S(1)} %copy.7, s32[]{:T(128)} %constant.3.clone.1, s32[]{:T(128)} %constant.3.clone.1, s32[]{:T(128)S(6)} %select_n.3, s32[]{:T(128)} %constant.3.clone.1) | dynamic-update-slice | bytes 196612 | tf_op jit(solution)/shard_map/dynamic_update_slice | solution.py:50
  11.6 45.0 %all-gather.3.cloned.1.call-done = bf16[2,1024,768]{2,1,0:T(8,128)(2,1)} async-done(((bf16[2,1024,384]{2,1,0:T(8,128)(2,1)}), bf16[2,1024,768]{2,1,0:T(8,128)(2,1)}) %all-gather.3.cloned.1.call-update) | async-done | bytes 3145744 | tf_op jit(solution)/shard_map/all_gather | solution.py:43
  56.6 2.3 fusion.1
  59.1 0.3 copy-done.5
  59.4 0.6 fusion.4
  60.0 0.3 copy.8
  60.3 2.3 fusion
  62.8 0.3 copy-done.6
  63.1 1.5 fusion.5
  64.6 1.4 copy.9
  66.0 1.4 maximum_subtract_fusion
  67.4 0.7 all-gather.5.cloned.1.call-update
  68.1 94.8 %all-reduce.2.cloned.1.call-done = f32[2,3,256,256]{2,3,0,1:T(8,128)} async-done(((f32[2,3,256,256]{2,3,0,1:T(8,128)}), f32[2,3,256,256]{2,3,0,1:T(8,128)}) %all-reduce.2.cloned.1.call-update) | async-done | bytes 1572880 | tf_op jit(solution)/shard_map/psum | solution.py:53
  162.9 1.2 fusion.32
  164.1 1.3 fusion.17
  165.4 1.2 fusion.33
  166.7 1.3 fusion.16
  168.0 20.1 %all_gather.13 = bf16[2,256,256]{2,1,0:T(8,128)(2,1)S(1)} all-gather(bf16[2,16,256]{2,1,0:T(8,128)(2,1)S(1)} %fusion.47), channel_id=1, replica_groups=mesh['row'=16,'col'=2] {'row'}, dimensions={1}, use_global_device_ids=true | all-gather | bytes 278528 | tf_op jit(solution)/shard_map/all_gather | solution.py:66
  188.1 18.7 %all-gather.5.cloned.1.call-done = bf16[3,2,256,768]{3,2,1,0:T(8,128)(2,1)} async-done(((bf16[3,2,16,768]{3,2,1,0:T(8,128)(2,1)}), bf16[3,2,256,768]{3,2,1,0:T(8,128)(2,1)}) %all-gather.5.cloned.1.call-update) | async-done | bytes 2359312 | tf_op jit(solution)/shard_map/all_gather | solution.py:54
  206.8 1.5 slice_bitcast_fusion.10
  210.0 0.3 fusion.34
  210.3 0.3 fusion.35
  210.6 0.3 fusion.15
  210.9 0.3 fusion.14
  211.3 19.9 %all_gather.15 = bf16[2,256,256]{2,1,0:T(8,128)(2,1)S(1)} all-gather(bf16[2,16,256]{2,1,0:T(8,128)(2,1)S(1)} %fusion.45), channel_id=1, replica_groups=mesh['row'=16,'col'=2] {'row'}, dimensions={1}, use_global_device_ids=true | all-gather | bytes 278528 | tf_op jit(solution)/shard_map/all_gather | solution.py:66
  232.7 0.3 fusion.36
  233.0 0.3 fusion.37
  233.4 0.3 fusion.13
  233.7 0.3 fusion.12
  234.1 0.6 pad_maximum_fusion
  (39 shorter events, 4.4 us)
Async XLA Ops:
  6.5 0.9 copy-start
  6.5 0.9 copy-start.7
  6.5 50.0 %all-gather.3.cloned.1.call-start = ((), (), s32[]{:S(2)}) async-start(), calls=%async_computation | async-start | bytes 4718592 | tf_op jit(solution)/shard_map/all_gather | solution.py:43
  7.3 155.6 %all-reduce.2.cloned.1.call-start = ((), (), s32[]{:S(2)}) async-start(), calls=%async_computation.1 | async-start | bytes 3145728 | tf_op jit(solution)/shard_map/psum | solution.py:53
  56.6 2.5 %copy-start.3 = (bf16[2,1024,768]{2,1,0:T(8,128)(2,1)S(1)}, bf16[2,1024,768]{2,1,0:T(8,128)(2,1)}, u32[]{:S(2)}) copy-start(bf16[2,1024,768]{2,1,0:T(8,128)(2,1)} %all-gather.3.cloned.1.call-done) | copy-start | bytes 9437188
  56.6 2.8 %copy-start.5 = (bf16[2,1024,256]{2,1,0:T(8,128)(2,1)S(1)}, bf16[2,1024,256]{2,1,0:T(8,128)(2,1)}, u32[]{:S(2)}) copy-start(bf16[2,1024,256]{2,1,0:T(8,128)(2,1)} %param.7) | copy-start | bytes 3145732
  60.3 2.5 %copy-start.4 = (bf16[2,1024,768]{2,1,0:T(8,128)(2,1)S(1)}, bf16[2,1024,768]{2,1,0:T(8,128)(2,1)}, u32[]{:S(2)}) copy-start(bf16[2,1024,768]{2,1,0:T(8,128)(2,1)} %all-gather.3.cloned.1.call-done) | copy-start | bytes 9437188
  60.3 2.8 %copy-start.6 = (bf16[2,1024,256]{2,1,0:T(8,128)(2,1)S(1)}, bf16[2,1024,256]{2,1,0:T(8,128)(2,1)}, u32[]{:S(2)}) copy-start(bf16[2,1024,256]{2,1,0:T(8,128)(2,1)} %param.7) | copy-start | bytes 3145732
  67.4 95.5 %copy-start.2 = (f32[3,2,16,256]{3,2,1,0:T(8,128)S(1)}, f32[3,2,16,256]{3,2,1,0:T(8,128)}, u32[]{:S(2)}) copy-start(f32[3,2,16,256]{3,2,1,0:T(8,128)} %param.9) | copy-start | bytes 294916
  67.4 139.4 %all-gather.5.cloned.1.call-start = ((), (), s32[]{:S(2)}) async-start(), calls=%async_computation.2 | async-start | bytes 2506752 | tf_op jit(solution)/shard_map/all_gather | solution.py:54
  208.5 1.4 copy-start.1
Sparse Core Ops, SparseCore 0:
  8.9 47.6 all-gather.2
  67.5 95.3 all-reduce.1
  165.2 41.5 all-gather.4
where the time goes:
time: 242 us; the launch traced here: 241 us
  waiting for transfers between devices  160 us (66%)
  blocking collectives  40 us (17%)
  matrix products  17.2 us (7%)
  between operations  13.5 us (6%)
  local copies, waits for them, and re-layouts  8.32 us (3%)
    psum x1, waiting for transfers between devices, shards(): base_rhs = lax.psum(placed_all - partial_value, 'row')  94.8 us
    all_gather x1, waiting for transfers between devices, shards(): lax.all_gather(tail_factor, 'col', axis=2, tiled=True)  45 us
    all_gather x2, blocking collectives, shards(): lax.all_gather(rounded[panel_index], 'row', axis=1, tiled=True)  40 us
    all_gather x1, waiting for transfers between devices, shards(): whole_coupling = lax.all_gather(coupling, 'row', axis=2, tiled=True)  18.7 us
  transfers between devices with their start and end apart: 3, of which 3 were waited for; matrix products, arithmetic and copies ran while one was open for 4% of the time, Pallas kernels for 0%

commit v1 on v0

--- a/solution.py
+++ b/solution.py
@@ -1,7 +1,13 @@
+import functools
+
 import jax
 import jax.numpy as jnp
 from jax import lax
+from jax.experimental import pallas as pl
+from jax.experimental.pallas import tpu as pltpu
 from jax.sharding import PartitionSpec as P
+
+MESH = pl.DeviceIdType.MESH
 
 
 def conj_tproduct(factor_part, solution_part):
@@ -67,6 +73,329 @@
     return jnp.stack(solved)
 
 
+def split_two(value):
+    high = value.astype(jnp.bfloat16)
+    low = (value - high.astype(jnp.float32)).astype(jnp.bfloat16)
+    return high, low
+
+
+def dot_tn(left, right):
+    return lax.dot_general(
+        left, right, (((0,), (0,)), ((), ())), preferred_element_type=jnp.float32
+    )
+
+
+def dot_nt(left, right):
+    return lax.dot_general(
+        left, right, (((1,), (1,)), ((), ())), preferred_element_type=jnp.float32
+    )
+
+
+def dot_nn(left, right):
+    return lax.dot_general(
+        left, right, (((1,), (0,)), ((), ())), preferred_element_type=jnp.float32
+    )
+
+
+def panel_pairs(panels):
+    return [(j, k) for j in range(panels) for k in range(j)]
+
+
+def fused_kernel(
+    rows, depth, panels, chunks,
+    factor, tail, coupling, inverse, sources, station, out,
+    rx, part, core_in, core_sum, y_in, y_sum, z_in, reduced, x_in,
+    blocks, adj_out, adj_in, sol_out, xs, adj_s, sol_s, core_s, y_s, z_s, swap_s,
+    bz_s, by_s, bc_s,
+):
+    row = lax.axis_index("row")
+    col = lax.axis_index("col")
+    core = lax.rem(row, 2)
+    yy = lax.rem(row // 2, 2)
+    zz = row // 4
+    width = factor.shape[2]
+    local = inverse.shape[2]
+    panel = inverse.shape[3]
+    span = rows * 8
+    lanes = adj_in.shape[3]
+    kinds = panels * 2
+
+    def slot_of(r):
+        return (lax.rem(r, 2) * 2 + lax.rem(r // 2, 2)) * depth + r // 4
+
+    def row_of(z, y, c):
+        return z * 4 + y * 2 + c
+
+    my_slot = slot_of(row)
+    peers = [lax.rem(row + d, rows) for d in range(1, rows)]
+    core_peer = row_of(zz, yy, 1 - core)
+    y_peer = row_of(zz, 1 - yy, core)
+    z_hops = [lax.rem(zz + d, depth) for d in range(1, depth)]
+    z_from = [lax.rem(zz + depth - d, depth) for d in range(1, depth)]
+    pending = []
+
+    def send(source, target, sems, device_row, device_col, *index):
+        copy = pltpu.make_async_remote_copy(
+            src_ref=source, dst_ref=target,
+            send_sem=sems.at[(0, *index)], recv_sem=sems.at[(1, *index)],
+            device_id=(device_row, device_col), device_id_type=MESH,
+        )
+        copy.start()
+        pending.append(copy)
+        return copy
+
+    barrier = pltpu.get_barrier_semaphore()
+    for peer in peers:
+        pl.semaphore_signal(barrier, inc=1, device_id=(peer, col), device_id_type=MESH)
+    pl.semaphore_signal(barrier, inc=1, device_id=(row, 1 - col), device_id_type=MESH)
+    pl.semaphore_wait(barrier, rows)
+
+    x_copies = [
+        send(tail.at[:, :, pl.ds(q * span, span)], rx.at[q], xs, row, 1 - col, q)
+        for q in range(chunks)
+    ]
+
+    pairs = panel_pairs(panels)
+    for k in range(panels):
+        for c in range(2):
+            high, low = split_two(inverse[k, c])
+            blocks[row, k * 2 + c] = high
+            blocks[row, kinds + k * 2 + c] = low
+    for place, (j, k) in enumerate(pairs):
+        for c in range(2):
+            blocks[row, 2 * kinds + place * 2 + c] = coupling[
+                j, c, :, k * panel:(k + 1) * panel
+            ]
+    bz = [
+        send(blocks.at[row], blocks.at[row], bz_s, row_of(z, yy, core), col, d)
+        for d, z in enumerate(z_hops)
+    ]
+    by = [send(blocks.at[row], blocks.at[row], by_s, y_peer, col, 0)]
+    bc = [send(blocks.at[row], blocks.at[row], bc_s, core_peer, col, 0)]
+
+    def multiply(real, imag):
+        re = dot_tn(real, factor[0]) + dot_tn(imag, factor[1])
+        im = dot_tn(imag, factor[0]) - dot_tn(real, factor[1])
+        return re, im
+
+    core_copies, y_copies, z_copies = {}, {}, {}
+
+    def stage_core(chunk, real, imag):
+        re, im = multiply(real, imag)
+        shape = (2, 2, depth, 8, width)
+        part[chunk, :, :, :, :, 0:width] = re.reshape(shape)
+        part[chunk, :, :, :, :, width:2 * width] = im.reshape(shape)
+        core_copies[chunk] = send(
+            part.at[chunk, 1 - core], core_in.at[chunk], core_s, core_peer, col, chunk
+        )
+
+    def stage_y(chunk):
+        core_copies[chunk].wait_recv()
+        core_sum[chunk] = part[chunk, core] + core_in[chunk]
+        y_copies[chunk] = send(
+            core_sum.at[chunk, 1 - yy], y_in.at[chunk], y_s, y_peer, col, chunk
+        )
+
+    def stage_z(chunk):
+        y_copies[chunk].wait_recv()
+        y_sum[chunk] = core_sum[chunk, yy] + y_in[chunk]
+        z_copies[chunk] = [
+            send(y_sum.at[chunk, z], z_in.at[chunk, d], z_s, row_of(z, yy, core), col, chunk, d)
+            for d, z in enumerate(z_hops)
+        ]
+
+    def stage_end(chunk):
+        total = y_sum[chunk, zz]
+        for d, copy in enumerate(z_copies[chunk]):
+            copy.wait_recv()
+            total = total + z_in[chunk, d]
+        reduced[chunk] = total
+
+    for q in range(chunks):
+        stage_core(q, tail[0, :, q * span:(q + 1) * span], tail[1, :, q * span:(q + 1) * span])
+
+    count = sources.shape[3]
+    selector = (
+        lax.broadcasted_iota(jnp.int32, (count, tail.shape[2]), 0) == station[...]
+    ).astype(jnp.float32).astype(jnp.bfloat16)
+    flat = sources[...].reshape(kinds * local, count)
+    if lanes > kinds * local:
+        flat = jnp.concatenate(
+            [flat, jnp.zeros((lanes - kinds * local, count), jnp.float32)], axis=0
+        )
+    first, rest = split_two(flat)
+    rest = flat - first.astype(jnp.float32)
+    second, third = split_two(rest)
+    taken = dot_tn(selector, jnp.transpose(first)) + dot_tn(selector, jnp.transpose(second))
+    taken = taken + dot_tn(selector, jnp.transpose(third))
+    for q in range(chunks):
+        adj_out[:, q] = taken[q * span:(q + 1) * span].reshape(rows, 8, lanes)
+    adj_copies = [
+        send(adj_out.at[slot_of(peer)], adj_in.at[row], adj_s, peer, col, d)
+        for d, peer in enumerate(peers)
+    ]
+    adj_in[row] = adj_out[my_slot]
+
+    for q in range(chunks):
+        stage_y(q)
+    for d in range(depth - 1):
+        bz[d].wait_recv()
+        place = blocks.at[row_of(z_from[d], yy, core)]
+        by.append(send(place, place, by_s, y_peer, col, d + 1))
+        bc.append(send(place, place, bc_s, core_peer, col, d + 1))
+    for q in range(chunks):
+        stage_z(q)
+    for d, z in enumerate([zz] + z_from):
+        by[d].wait_recv()
+        place = blocks.at[row_of(z, 1 - yy, core)]
+        bc.append(send(place, place, bc_s, core_peer, col, depth + d))
+    for q in range(chunks):
+        stage_end(q)
+
+    for copy in adj_copies:
+        copy.wait_recv()
+    received = [adj_in[r].reshape(chunks * 8, lanes) for r in range(rows)]
+    adjoint = [
+        jnp.concatenate([piece[:, n * local:(n + 1) * local] for piece in received], axis=1)
+        for n in range(kinds)
+    ]
+
+    for q in range(chunks):
+        x_copies[q].wait_recv()
+        stage_core(chunks + q, rx[q, 0], rx[q, 1])
+        if q > 0:
+            stage_z(chunks + q - 1)
+        stage_y(chunks + q)
+    for copy in bc:
+        copy.wait_recv()
+    stage_z(2 * chunks - 1)
+    swaps = []
+    for q in range(chunks):
+        stage_end(chunks + q)
+        swaps.append(send(reduced.at[chunks + q], x_in.at[q], swap_s, row, 1 - col, q))
+    for copy in swaps:
+        copy.wait_recv()
+
+    own = reduced[0:chunks].reshape(chunks * 8, 2 * width)
+    other = x_in[...].reshape(chunks * 8, 2 * width)
+    lower = jnp.where(col == 0, own, other)
+    upper = jnp.where(col == 0, other, own)
+    sums = [
+        jnp.concatenate([lower[:, c * width:(c + 1) * width], upper[:, c * width:(c + 1) * width]], axis=1)
+        for c in range(2)
+    ]
+
+    def block(n):
+        return blocks[:, n].reshape(panel, panel)
+
+    count_r = chunks * 8
+    rounded = [None] * panels
+    solved = [None] * kinds
+    for k in range(panels - 1, -1, -1):
+        real = sums[0][:, k * panel:(k + 1) * panel]
+        imag = sums[1][:, k * panel:(k + 1) * panel]
+        for j in range(k + 1, panels):
+            place = 2 * kinds + pairs.index((j, k)) * 2
+            with_real = dot_nn(rounded[j], block(place))
+            with_imag = dot_nn(rounded[j], block(place + 1))
+            real = real + with_real[:count_r] + with_imag[count_r:]
+            imag = imag + with_real[count_r:] - with_imag[:count_r]
+        residue = jnp.concatenate([adjoint[k * 2] - real, adjoint[k * 2 + 1] - imag], axis=0)
+        high, low = split_two(residue)
+        both = jnp.concatenate([high, low], axis=0)
+        products = []
+        for c in range(2):
+            wide = dot_nt(both, block(k * 2 + c))
+            fine = dot_nt(high, block(kinds + k * 2 + c))
+            products.append(wide[:2 * count_r] + wide[2 * count_r:] + fine)
+        solved[k * 2] = products[0][:count_r] - products[1][count_r:]
+        solved[k * 2 + 1] = products[0][count_r:] + products[1][:count_r]
+        rounded[k] = jnp.concatenate([solved[k * 2], solved[k * 2 + 1]], axis=0).astype(jnp.bfloat16)
+    filler = [jnp.zeros((count_r, lanes - kinds * local), jnp.float32)] if lanes > kinds * local else []
+    for r in range(rows):
+        pieces = [value[:, r * local:(r + 1) * local] for value in solved] + filler
+        sol_out[r] = jnp.concatenate(pieces, axis=1).reshape(chunks, 8, lanes)
+    sol_copies = [
+        send(sol_out.at[peer], out.at[my_slot], sol_s, peer, col, d)
+        for d, peer in enumerate(peers)
+    ]
+    out[my_slot] = sol_out[row]
+    for copy in sol_copies:
+        copy.wait_recv()
+    for copy in pending:
+        copy.wait_send()
+
+
+def fused_shards(rows, tail_factor, tail_solution, coupling, inverse_blocks, sources, station_map):
+    panels, _, local, panel = inverse_blocks.shape
+    depth = rows // 4
+    width = tail_factor.shape[2]
+    rhs = tail_solution.shape[2]
+    tall = tail_solution.shape[1]
+    chunks = rhs // (rows * 8)
+    lanes = -(-panels * 2 * local // 128) * 128
+    kept = 4 * panels + panels * (panels - 1)
+    vmem = pl.BlockSpec(memory_space=pltpu.VMEM)
+    f32, bf16 = jnp.float32, jnp.bfloat16
+    sem = pltpu.SemaphoreType.DMA
+    gathered = pl.pallas_call(
+        functools.partial(fused_kernel, rows, depth, panels, chunks),
+        out_shape=jax.ShapeDtypeStruct((rows, chunks, 8, lanes), f32),
+        in_specs=[vmem] * 6,
+        out_specs=vmem,
+        scratch_shapes=[
+            pltpu.VMEM((chunks, 2, tall, rows * 8), bf16),
+            pltpu.VMEM((2 * chunks, 2, 2, depth, 8, 2 * width), f32),
+            pltpu.VMEM((2 * chunks, 2, depth, 8, 2 * width), f32),
+            pltpu.VMEM((2 * chunks, 2, depth, 8, 2 * width), f32),
+            pltpu.VMEM((2 * chunks, depth, 8, 2 * width), f32),
+            pltpu.VMEM((2 * chunks, depth, 8, 2 * width), f32),
+            pltpu.VMEM((2 * chunks, depth - 1, 8, 2 * width), f32),
+            pltpu.VMEM((2 * chunks, 8, 2 * width), f32),
+            pltpu.VMEM((chunks, 8, 2 * width), f32),
+            pltpu.VMEM((rows, kept, local, panel), bf16),
+            pltpu.VMEM((rows, chunks, 8, lanes), f32),
+            pltpu.VMEM((rows, chunks, 8, lanes), f32),
+            pltpu.VMEM((rows, chunks, 8, lanes), f32),
+            sem((2, chunks)),
+            sem((2, rows - 1)),
+            sem((2, rows - 1)),
+            sem((2, 2 * chunks)),
+            sem((2, 2 * chunks)),
+            sem((2, 2 * chunks, depth - 1)),
+            sem((2, chunks)),
+            sem((2, depth - 1)),
+            sem((2, depth)),
+            sem((2, 2 * depth)),
+        ],
+        compiler_params=pltpu.CompilerParams(
+            collective_id=0, has_side_effects=True, vmem_limit_bytes=40 * 1024 * 1024
+        ),
+    )(tail_factor, tail_solution, coupling, inverse_blocks, sources, station_map[None, :])
+    used = gathered[..., : panels * 2 * local].reshape(rows, chunks, 8, panels, 2, local)
+    return jnp.transpose(used, (3, 4, 5, 1, 0, 2)).reshape(panels, 2, local, rhs)
+
+
+def plan(mesh):
+    rows, cols = mesh.shape["row"], mesh.shape["col"]
+
+    def body(tail_factor, tail_solution, coupling, inverse_blocks, sources, station_map):
+        fits = (
+            cols == 2
+            and rows % 4 == 0
+            and rows >= 8
+            and tail_factor.shape[2] % 128 == 0
+            and (rows * 8) % 128 == 0
+            and tail_solution.shape[2] % (rows * 8) == 0
+            and inverse_blocks.shape[2] % 16 == 0
+            and inverse_blocks.shape[3] % 128 == 0
+        )
+        arrays = (tail_factor, tail_solution, coupling, inverse_blocks, sources, station_map)
+        return fused_shards(rows, *arrays) if fits else shards(*arrays)
+
+    return body
+
+
 def solution(mesh):
     placed = (
         P(None, "row", "col"),
@@ -77,5 +406,5 @@
         P("col"),
     )
     return jax.shard_map(
-        shards, mesh=mesh, in_specs=placed, out_specs=P(None, None, "row", "col"), check_vma=False
-    )
+        plan(mesh), mesh=mesh, in_specs=placed, out_specs=P(None, None, "row", "col"), check_vma=False
+    )

time: 242 us -> 62.9 us (0.26)
  waiting for transfers between devices: 160 us -> 0 us
  Pallas kernels: 0 us -> 55.1 us
  blocking collectives: 40 us -> 0 us
  matrix products: 17.2 us -> 0 us
  between operations: 13.5 us -> 0.03 us
    psum x1 -> x0, waiting for transfers between devices: 94.8 us -> none  [shards(): base_rhs = lax.psum(placed_all - partial_value, 'row')]
    all_gather x2 -> x0, waiting for transfers between devices: 63.7 us -> none  [the longest x1 45 us: shards(): lax.all_gather(tail_factor, 'col', axis=2, tiled=True)]
    pallas_call x0 -> x1, Pallas kernels: none -> 55.1 us  [fused_shards(): pl.pallas_call(functools.partial(fused_kernel, rows, depth, panels, chunk...]
    all_gather x2 -> x0, blocking collectives: 40 us -> none  [shards(): lax.all_gather(rounded[panel_index], 'row', axis=1, tiled=True)]
    dot_general x29 -> x0, matrix products: 17.2 us -> none  [the longest x4 2.94 us: conj_tproduct(): jnp.einsum('pq,pr->qr', factor_part[0], solution_part[1], preferred_eleme...]
    unnamed x16 -> x12, local copies, waits for them, and re-layouts: 1.42 us -> 6.04 us
    dynamic_update_slice x1 -> x0, local copies, waits for them, and re-layouts: 3.38 us -> none  [shards(): lax.dynamic_update_slice_in_dim(jnp.zeros_like(partial_value), own_rhs, r...]
  transfers between devices with their start and end apart: 3 -> 0, of which waited for: 3 -> 0; matrix products, arithmetic and copies ran while one was open for 4% -> 0% of each run, Pallas kernels for 0% -> 0%
where the time goes in v1:
time: 62.9 us; the launch traced here: 62.6 us
  Pallas kernels  55.1 us (88%)
  local copies, waits for them, and re-layouts  7.52 us (12%)
    pallas_call x1, Pallas kernels, fused_shards(): pl.pallas_call(functools.partial(fused_kernel, rows, depth, panels, chunk...  55.1 us
    unnamed x12, local copies, waits for them, and re-layouts  6.04 us

profile of v1, /device:TPU:0, one launch (start us, length us, event | category | flops | bytes accessed | tf_op | source)
XLA Modules:
  0.0 62.6 jit_solution(7717518946682992056)
XLA Ops:
  0.0 0.0 copy-start
  0.0 1.4 %copy-done = bf16[2,1024,384]{2,1,0:T(8,128)(2,1)S(1)} copy-done((bf16[2,1024,384]{2,1,0:T(8,128)(2,1)S(1)}, bf16[2,1024,384]{2,1,0:T(8,128)(2,1)}, u32[]{:S(2)}) %copy-start) | copy-done | bytes 1572888
  1.4 0.0 copy-start.1
  1.4 1.2 %copy-done.1 = bf16[2,1024,256]{2,1,0:T(8,128)(2,1)S(1)} copy-done((bf16[2,1024,256]{2,1,0:T(8,128)(2,1)S(1)}, bf16[2,1024,256]{2,1,0:T(8,128)(2,1)}, u32[]{:S(2)}) %copy-start.1) | copy-done | bytes 1048600
  2.6 0.0 copy-start.2
  2.6 0.9 %copy-done.2 = f32[3,2,16,512]{3,2,1,0:T(8,128)S(1)} copy-done((f32[3,2,16,512]{3,2,1,0:T(8,128)S(1)}, f32[3,2,16,512]{3,2,1,0:T(8,128)}, u32[]{:S(2)}) %copy-start.2) | copy-done | bytes 196632
  3.6 0.0 copy-start.3
  3.6 0.9 %copy-done.3 = bf16[3,2,16,768]{3,2,1,0:T(8,128)(2,1)S(1)} copy-done((bf16[3,2,16,768]{3,2,1,0:T(8,128)(2,1)S(1)}, bf16[3,2,16,768]{3,2,1,0:T(8,128)(2,1)}, u32[]{:S(2)}) %copy-start.3) | copy-done | bytes 147480
  4.5 0.0 copy-start.4
  4.5 0.9 %copy-done.4 = f32[3,2,16,256]{3,2,1,0:T(8,128)S(1)} copy-done((f32[3,2,16,256]{3,2,1,0:T(8,128)S(1)}, f32[3,2,16,256]{3,2,1,0:T(8,128)}, u32[]{:S(2)}) %copy-start.4) | copy-done | bytes 98328
  5.4 0.0 copy-start.5
  5.4 0.7 %copy-done.5 = s32[256]{0:T(256)S(1)} copy-done((s32[256]{0:T(256)S(1)}, s32[256]{0:T(256)}, u32[]{:S(2)}) %copy-start.5) | copy-done | bytes 1048
  6.0 55.1 %shard_map.64 = f32[16,2,8,128]{3,2,1,0:T(8,128)S(1)} custom-call(bf16[2,1024,384]{2,1,0:T(8,128)(2,1)S(1)} %copy-done, bf16[2,1024,256]{2,1,0:T(8,128)(2,1)S(1)} %copy-done.1, bf16[3,2,16,768]{3,2,1,0:T(8,128)(2,1)S(1)} %copy-done.3, f32[3,2,16,256]{3,2,1,0:T(8,128)S(1)} %copy-done.4, f32[3,2,16,512]{3,2,1,0:T(8,128)S(1)} %copy-done.2, s32[1,256]{1,0:T(1,128)S(1)} %bitcast.8), custom_call_target="tpu_custom_call" | custom-call | tf_op jit(solution)/shard_map/pallas_call | solution.py:341
  61.1 0.5 reshape.6
  61.7 0.1 copy.8
  61.8 0.9 %copy.9 = f32[3,2,16,256]{3,2,1,0:T(8,128)} copy(f32[3,2,16,256]{2,3,1,0:T(8,128)S(1)} %bitcast.9) | data formatting | bytes 196608 | tf_op jit(solution)/shard_map/reshape | solution.py:376
Async XLA Ops:
  0.0 1.4 %copy-start = (bf16[2,1024,384]{2,1,0:T(8,128)(2,1)S(1)}, bf16[2,1024,384]{2,1,0:T(8,128)(2,1)}, u32[]{:S(2)}) copy-start(bf16[2,1024,384]{2,1,0:T(8,128)(2,1)} %factor.1) | copy-start | bytes 4718596
  1.4 1.2 %copy-start.1 = (bf16[2,1024,256]{2,1,0:T(8,128)(2,1)S(1)}, bf16[2,1024,256]{2,1,0:T(8,128)(2,1)}, u32[]{:S(2)}) copy-start(bf16[2,1024,256]{2,1,0:T(8,128)(2,1)} %tail.1) | copy-start | bytes 3145732
  2.6 0.9 %copy-start.2 = (f32[3,2,16,512]{3,2,1,0:T(8,128)S(1)}, f32[3,2,16,512]{3,2,1,0:T(8,128)}, u32[]{:S(2)}) copy-start(f32[3,2,16,512]{3,2,1,0:T(8,128)} %sources.1) | copy-start | bytes 589828
  3.6 0.9 %copy-start.3 = (bf16[3,2,16,768]{3,2,1,0:T(8,128)(2,1)S(1)}, bf16[3,2,16,768]{3,2,1,0:T(8,128)(2,1)}, u32[]{:S(2)}) copy-start(bf16[3,2,16,768]{3,2,1,0:T(8,128)(2,1)} %coupling.1) | copy-start | bytes 442372
  4.5 0.9 %copy-start.4 = (f32[3,2,16,256]{3,2,1,0:T(8,128)S(1)}, f32[3,2,16,256]{3,2,1,0:T(8,128)}, u32[]{:S(2)}) copy-start(f32[3,2,16,256]{3,2,1,0:T(8,128)} %inverse.1) | copy-start | bytes 294916
  5.4 0.7 %copy-start.5 = (s32[256]{0:T(256)S(1)}, s32[256]{0:T(256)}, u32[]{:S(2)}) copy-start(s32[256]{0:T(256)} %param.11) | copy-start | bytes 3076

commit v2 on v1

--- a/solution.py
+++ b/solution.py
@@ -103,10 +103,10 @@
 
 def fused_kernel(
     rows, depth, panels, chunks,
-    factor, tail, coupling, inverse, sources, station, out,
-    rx, part, core_in, core_sum, y_in, y_sum, z_in, reduced, x_in,
-    blocks, adj_out, adj_in, sol_out, xs, adj_s, sol_s, core_s, y_s, z_s, swap_s,
-    bz_s, by_s, bc_s,
+    factor_h, tail_h, coupling_h, inverse_h, sources_h, station_h, out,
+    factor, tail, coupling, inverse, sources, station, rx, part, core_in, core_sum, y_in, y_sum, z_in, reduced, far_in,
+    blocks, adj_out, adj_in, sol_out, xs, adj_s, sol_s, core_s, y_s, z_s, far_s,
+    bz_s, by_s, bc_s, load_s,
 ):
     row = lax.axis_index("row")
     col = lax.axis_index("col")
@@ -144,17 +144,24 @@
         pending.append(copy)
         return copy
 
+    loads = []
+    for n, (source, target) in enumerate((
+        (inverse_h, inverse), (coupling_h, coupling), (tail_h, tail),
+        (factor_h, factor), (sources_h, sources), (station_h, station),
+    )):
+        load = pltpu.make_async_copy(source, target, load_s.at[n])
+        load.start()
+        loads.append(load)
     barrier = pltpu.get_barrier_semaphore()
     for peer in peers:
         pl.semaphore_signal(barrier, inc=1, device_id=(peer, col), device_id_type=MESH)
-    pl.semaphore_signal(barrier, inc=1, device_id=(row, 1 - col), device_id_type=MESH)
-    pl.semaphore_wait(barrier, rows)
-
-    x_copies = [
-        send(tail.at[:, :, pl.ds(q * span, span)], rx.at[q], xs, row, 1 - col, q)
-        for q in range(chunks)
-    ]
-
+    for z in [zz] + z_hops:
+        pl.semaphore_signal(
+            barrier, inc=1, device_id=(row_of(z, yy, core), 1 - col), device_id_type=MESH
+        )
+
+    loads[0].wait()
+    loads[1].wait()
     pairs = panel_pairs(panels)
     for k in range(panels):
         for c in range(2):
@@ -166,6 +173,13 @@
             blocks[row, 2 * kinds + place * 2 + c] = coupling[
                 j, c, :, k * panel:(k + 1) * panel
             ]
+    pl.semaphore_wait(barrier, rows - 1 + depth)
+
+    def send_x(q):
+        return send(tail_h.at[:, :, pl.ds(q * span, span)], rx.at[q], xs, row, 1 - col, q)
+
+    x_copies = [send_x(0)]
+
     bz = [
         send(blocks.at[row], blocks.at[row], bz_s, row_of(z, yy, core), col, d)
         for d, z in enumerate(z_hops)
@@ -199,6 +213,15 @@
     def stage_z(chunk):
         y_copies[chunk].wait_recv()
         y_sum[chunk] = core_sum[chunk, yy] + y_in[chunk]
+        if chunk >= chunks:
+            z_copies[chunk] = [
+                send(
+                    y_sum.at[chunk, z], far_in.at[chunk - chunks, d], far_s,
+                    row_of(z, yy, core), 1 - col, chunk - chunks, d,
+                )
+                for d, z in enumerate([zz] + z_hops)
+            ]
+            return
         z_copies[chunk] = [
             send(y_sum.at[chunk, z], z_in.at[chunk, d], z_s, row_of(z, yy, core), col, chunk, d)
             for d, z in enumerate(z_hops)
@@ -211,9 +234,13 @@
             total = total + z_in[chunk, d]
         reduced[chunk] = total
 
+    loads[2].wait()
+    loads[3].wait()
     for q in range(chunks):
         stage_core(q, tail[0, :, q * span:(q + 1) * span], tail[1, :, q * span:(q + 1) * span])
 
+    loads[4].wait()
+    loads[5].wait()
     count = sources.shape[3]
     selector = (
         lax.broadcasted_iota(jnp.int32, (count, tail.shape[2]), 0) == station[...]
@@ -236,6 +263,7 @@
     ]
     adj_in[row] = adj_out[my_slot]
 
+    x_copies += [send_x(q) for q in range(1, chunks)]
     for q in range(chunks):
         stage_y(q)
     for d in range(depth - 1):
@@ -245,39 +273,41 @@
         bc.append(send(place, place, bc_s, core_peer, col, d + 1))
     for q in range(chunks):
         stage_z(q)
-    for d, z in enumerate([zz] + z_from):
-        by[d].wait_recv()
-        place = blocks.at[row_of(z, 1 - yy, core)]
-        bc.append(send(place, place, bc_s, core_peer, col, depth + d))
-    for q in range(chunks):
-        stage_end(q)
-
-    for copy in adj_copies:
-        copy.wait_recv()
-    received = [adj_in[r].reshape(chunks * 8, lanes) for r in range(rows)]
-    adjoint = [
-        jnp.concatenate([piece[:, n * local:(n + 1) * local] for piece in received], axis=1)
-        for n in range(kinds)
-    ]
 
     for q in range(chunks):
         x_copies[q].wait_recv()
         stage_core(chunks + q, rx[q, 0], rx[q, 1])
-        if q > 0:
-            stage_z(chunks + q - 1)
+        if q == 0:
+            for own_chunk in range(chunks):
+                stage_end(own_chunk)
         stage_y(chunks + q)
+        stage_z(chunks + q)
+        if q == 0:
+            for copy in adj_copies:
+                copy.wait_recv()
+            received = [adj_in[r].reshape(chunks * 8, lanes) for r in range(rows)]
+            adjoint = [
+                jnp.concatenate(
+                    [piece[:, n * local:(n + 1) * local] for piece in received], axis=1
+                )
+                for n in range(kinds)
+            ]
+            for d, z in enumerate([zz] + z_from):
+                by[d].wait_recv()
+                place = blocks.at[row_of(z, 1 - yy, core)]
+                bc.append(send(place, place, bc_s, core_peer, col, depth + d))
     for copy in bc:
         copy.wait_recv()
-    stage_z(2 * chunks - 1)
-    swaps = []
-    for q in range(chunks):
-        stage_end(chunks + q)
-        swaps.append(send(reduced.at[chunks + q], x_in.at[q], swap_s, row, 1 - col, q))
-    for copy in swaps:
-        copy.wait_recv()
+    others = []
+    for q in range(chunks):
+        total = None
+        for d, copy in enumerate(z_copies[chunks + q]):
+            copy.wait_recv()
+            total = far_in[q, d] if total is None else total + far_in[q, d]
+        others.append(total)
 
     own = reduced[0:chunks].reshape(chunks * 8, 2 * width)
-    other = x_in[...].reshape(chunks * 8, 2 * width)
+    other = jnp.concatenate(others, axis=0)
     lower = jnp.where(col == 0, own, other)
     upper = jnp.where(col == 0, other, own)
     sums = [
@@ -341,18 +371,24 @@
     gathered = pl.pallas_call(
         functools.partial(fused_kernel, rows, depth, panels, chunks),
         out_shape=jax.ShapeDtypeStruct((rows, chunks, 8, lanes), f32),
-        in_specs=[vmem] * 6,
+        in_specs=[pl.BlockSpec(memory_space=pltpu.HBM)] * 6,
         out_specs=vmem,
         scratch_shapes=[
+            pltpu.VMEM(tail_factor.shape, bf16),
+            pltpu.VMEM(tail_solution.shape, bf16),
+            pltpu.VMEM(coupling.shape, bf16),
+            pltpu.VMEM(inverse_blocks.shape, f32),
+            pltpu.VMEM(sources.shape, f32),
+            pltpu.VMEM((1, rhs), jnp.int32),
             pltpu.VMEM((chunks, 2, tall, rows * 8), bf16),
             pltpu.VMEM((2 * chunks, 2, 2, depth, 8, 2 * width), f32),
             pltpu.VMEM((2 * chunks, 2, depth, 8, 2 * width), f32),
             pltpu.VMEM((2 * chunks, 2, depth, 8, 2 * width), f32),
             pltpu.VMEM((2 * chunks, depth, 8, 2 * width), f32),
             pltpu.VMEM((2 * chunks, depth, 8, 2 * width), f32),
-            pltpu.VMEM((2 * chunks, depth - 1, 8, 2 * width), f32),
-            pltpu.VMEM((2 * chunks, 8, 2 * width), f32),
+            pltpu.VMEM((chunks, depth - 1, 8, 2 * width), f32),
             pltpu.VMEM((chunks, 8, 2 * width), f32),
+            pltpu.VMEM((chunks, depth, 8, 2 * width), f32),
             pltpu.VMEM((rows, kept, local, panel), bf16),
             pltpu.VMEM((rows, chunks, 8, lanes), f32),
             pltpu.VMEM((rows, chunks, 8, lanes), f32),
@@ -362,14 +398,15 @@
             sem((2, rows - 1)),
             sem((2, 2 * chunks)),
             sem((2, 2 * chunks)),
-            sem((2, 2 * chunks, depth - 1)),
-            sem((2, chunks)),
+            sem((2, chunks, depth - 1)),
+            sem((2, chunks, depth)),
             sem((2, depth - 1)),
             sem((2, depth)),
             sem((2, 2 * depth)),
+            sem((6,)),
         ],
         compiler_params=pltpu.CompilerParams(
-            collective_id=0, has_side_effects=True, vmem_limit_bytes=40 * 1024 * 1024
+            collective_id=0, has_side_effects=True, vmem_limit_bytes=63 * 1024 * 1024
         ),
     )(tail_factor, tail_solution, coupling, inverse_blocks, sources, station_map[None, :])
     used = gathered[..., : panels * 2 * local].reshape(rows, chunks, 8, panels, 2, local)

time: 62.9 us -> 53.9 us (0.86)
  local copies, waits for them, and re-layouts: 7.52 us -> 2.38 us
  Pallas kernels: 55.1 us -> 51.3 us
    unnamed x12 -> x0, local copies, waits for them, and re-layouts: 6.04 us -> none
    pallas_call x1, Pallas kernels: 55.1 us -> 51.3 us  [fused_shards(): pl.pallas_call(functools.partial(fused_kernel, rows, depth, panels, chunk...]
    reshape x2, local copies, waits for them, and re-layouts: 0.6 us -> 1.5 us  [fused_shards(): gathered[..., :panels * 2 * local]]
where the time goes in v2:
time: 53.9 us; the launch traced here: 53.8 us
  Pallas kernels  51.3 us (95%)
  local copies, waits for them, and re-layouts  2.38 us (4%)
    pallas_call x1, Pallas kernels, fused_shards(): pl.pallas_call(functools.partial(fused_kernel, rows, depth, panels, chunk...  51.3 us
    reshape x2, local copies, waits for them, and re-layouts, fused_shards(): gathered[..., :panels * 2 * local]  1.5 us

profile of v2, /device:TPU:0, one launch (start us, length us, event | category | flops | bytes accessed | tf_op | source)
XLA Modules:
  0.0 53.8 jit_solution(9799994271069039348)
XLA Ops:
  0.0 51.3 %shard_map.64 = f32[16,2,8,128]{3,2,1,0:T(8,128)} custom-call(bf16[2,1024,384]{2,1,0:T(8,128)(2,1)} %factor_h.1, bf16[2,1024,256]{2,1,0:T(8,128)(2,1)} %tail_h.1, bf16[3,2,16,768]{3,2,1,0:T(8,128)(2,1)} %coupling_h.1, f32[3,2,16,256]{3,2,1,0:T(8,128)} %inverse_h.1, f32[3,2,16,512]{3,2,1,0:T(8,128)} %sources_h.1, s32[1,256]{1,0:T(1,128)} %bitcast.9), custom_call_target="tpu_custom_call" | custom-call | tf_op jit(solution)/shard_map/pallas_call | solution.py:371
  51.4 1.4 %reshape.6 = f32[16,2,8,3,2,16]{5,4,3,2,1,0:T(2,128)S(1)} reshape(f32[16,2,8,96]{3,2,1,0:T(8,128)} %bitcast.8) | data formatting | bytes 196608 | tf_op jit(solution)/shard_map/reshape | solution.py:412
  52.8 0.1 copy.8
  52.9 0.9 %copy.9 = f32[3,2,16,256]{3,2,1,0:T(8,128)} copy(f32[3,2,16,256]{2,3,1,0:T(8,128)S(1)} %bitcast.7) | data formatting | bytes 196608 | tf_op jit(solution)/shard_map/reshape | solution.py:413

commit v3 on v2

--- a/solution.py
+++ b/solution.py
@@ -105,6 +105,7 @@
     rows, depth, panels, chunks,
     factor_h, tail_h, coupling_h, inverse_h, sources_h, station_h, out,
     factor, tail, coupling, inverse, sources, station, rx, part, core_in, core_sum, y_in, y_sum, z_in, reduced, far_in,
+    core_low, y_low, z_low, sol_in,
     blocks, adj_out, adj_in, sol_out, xs, adj_s, sol_s, core_s, y_s, z_s, far_s,
     bz_s, by_s, bc_s, load_s,
 ):
@@ -197,8 +198,8 @@
     def stage_core(chunk, real, imag):
         re, im = multiply(real, imag)
         shape = (2, 2, depth, 8, width)
-        part[chunk, :, :, :, :, 0:width] = re.reshape(shape)
-        part[chunk, :, :, :, :, width:2 * width] = im.reshape(shape)
+        part[chunk, :, :, :, 0:8, :] = re.reshape(shape)
+        part[chunk, :, :, :, 8:16, :] = im.reshape(shape)
         core_copies[chunk] = send(
             part.at[chunk, 1 - core], core_in.at[chunk], core_s, core_peer, col, chunk
         )
@@ -206,22 +207,29 @@
     def stage_y(chunk):
         core_copies[chunk].wait_recv()
         core_sum[chunk] = part[chunk, core] + core_in[chunk]
+        if chunk >= chunks:
+            late = chunk - chunks
+            core_low[late] = core_sum[chunk, 1 - yy].astype(jnp.bfloat16)
+            y_copies[chunk] = send(core_low.at[late], y_low.at[late], y_s, y_peer, col, chunk)
+            return
         y_copies[chunk] = send(
             core_sum.at[chunk, 1 - yy], y_in.at[chunk], y_s, y_peer, col, chunk
         )
 
     def stage_z(chunk):
         y_copies[chunk].wait_recv()
-        y_sum[chunk] = core_sum[chunk, yy] + y_in[chunk]
         if chunk >= chunks:
+            late = chunk - chunks
+            z_low[late] = (core_sum[chunk, yy] + y_low[late].astype(jnp.float32)).astype(jnp.bfloat16)
             z_copies[chunk] = [
                 send(
-                    y_sum.at[chunk, z], far_in.at[chunk - chunks, d], far_s,
-                    row_of(z, yy, core), 1 - col, chunk - chunks, d,
+                    z_low.at[late, z], far_in.at[late, d], far_s,
+                    row_of(z, yy, core), 1 - col, late, d,
                 )
                 for d, z in enumerate([zz] + z_hops)
             ]
             return
+        y_sum[chunk] = core_sum[chunk, yy] + y_in[chunk]
         z_copies[chunk] = [
             send(y_sum.at[chunk, z], z_in.at[chunk, d], z_s, row_of(z, yy, core), col, chunk, d)
             for d, z in enumerate(z_hops)
@@ -303,17 +311,18 @@
         total = None
         for d, copy in enumerate(z_copies[chunks + q]):
             copy.wait_recv()
-            total = far_in[q, d] if total is None else total + far_in[q, d]
+            piece = far_in[q, d].astype(jnp.float32)
+            total = piece if total is None else total + piece
         others.append(total)
 
-    own = reduced[0:chunks].reshape(chunks * 8, 2 * width)
-    other = jnp.concatenate(others, axis=0)
-    lower = jnp.where(col == 0, own, other)
-    upper = jnp.where(col == 0, other, own)
-    sums = [
-        jnp.concatenate([lower[:, c * width:(c + 1) * width], upper[:, c * width:(c + 1) * width]], axis=1)
-        for c in range(2)
-    ]
+    owns = [reduced[q] for q in range(chunks)]
+    sums = []
+    for c in range(2):
+        own = jnp.concatenate([value[c * 8:(c + 1) * 8] for value in owns], axis=0)
+        other = jnp.concatenate([value[c * 8:(c + 1) * 8] for value in others], axis=0)
+        lower = jnp.where(col == 0, own, other)
+        upper = jnp.where(col == 0, other, own)
+        sums.append(jnp.concatenate([lower, upper], axis=1))
 
     def block(n):
         return blocks[:, n].reshape(panel, panel)
@@ -344,14 +353,20 @@
     filler = [jnp.zeros((count_r, lanes - kinds * local), jnp.float32)] if lanes > kinds * local else []
     for r in range(rows):
         pieces = [value[:, r * local:(r + 1) * local] for value in solved] + filler
-        sol_out[r] = jnp.concatenate(pieces, axis=1).reshape(chunks, 8, lanes)
+        sol_out[r] = jnp.concatenate(pieces, axis=1).astype(jnp.bfloat16)
     sol_copies = [
-        send(sol_out.at[peer], out.at[my_slot], sol_s, peer, col, d)
+        send(sol_out.at[peer], sol_in.at[my_slot], sol_s, peer, col, d)
         for d, peer in enumerate(peers)
     ]
-    out[my_slot] = sol_out[row]
+    sol_in[my_slot] = sol_out[row]
     for copy in sol_copies:
         copy.wait_recv()
+    found = sol_in[...].astype(jnp.float32)
+    for q in range(chunks):
+        turned = jnp.transpose(found[:, q * 8:(q + 1) * 8].reshape(span, lanes))
+        out[:, :, :, q * span:(q + 1) * span] = turned[:kinds * local].reshape(
+            panels, 2, local, span
+        )
     for copy in pending:
         copy.wait_send()
 
@@ -368,9 +383,9 @@
     vmem = pl.BlockSpec(memory_space=pltpu.VMEM)
     f32, bf16 = jnp.float32, jnp.bfloat16
     sem = pltpu.SemaphoreType.DMA
-    gathered = pl.pallas_call(
+    return pl.pallas_call(
         functools.partial(fused_kernel, rows, depth, panels, chunks),
-        out_shape=jax.ShapeDtypeStruct((rows, chunks, 8, lanes), f32),
+        out_shape=jax.ShapeDtypeStruct((panels, 2, local, rhs), f32),
         in_specs=[pl.BlockSpec(memory_space=pltpu.HBM)] * 6,
         out_specs=vmem,
         scratch_shapes=[
@@ -381,18 +396,22 @@
             pltpu.VMEM(sources.shape, f32),
             pltpu.VMEM((1, rhs), jnp.int32),
             pltpu.VMEM((chunks, 2, tall, rows * 8), bf16),
-            pltpu.VMEM((2 * chunks, 2, 2, depth, 8, 2 * width), f32),
-            pltpu.VMEM((2 * chunks, 2, depth, 8, 2 * width), f32),
-            pltpu.VMEM((2 * chunks, 2, depth, 8, 2 * width), f32),
-            pltpu.VMEM((2 * chunks, depth, 8, 2 * width), f32),
-            pltpu.VMEM((2 * chunks, depth, 8, 2 * width), f32),
-            pltpu.VMEM((chunks, depth - 1, 8, 2 * width), f32),
-            pltpu.VMEM((chunks, 8, 2 * width), f32),
-            pltpu.VMEM((chunks, depth, 8, 2 * width), f32),
+            pltpu.VMEM((2 * chunks, 2, 2, depth, 16, width), f32),
+            pltpu.VMEM((2 * chunks, 2, depth, 16, width), f32),
+            pltpu.VMEM((2 * chunks, 2, depth, 16, width), f32),
+            pltpu.VMEM((chunks, depth, 16, width), f32),
+            pltpu.VMEM((chunks, depth, 16, width), f32),
+            pltpu.VMEM((chunks, depth - 1, 16, width), f32),
+            pltpu.VMEM((chunks, 16, width), f32),
+            pltpu.VMEM((chunks, depth, 16, width), bf16),
+            pltpu.VMEM((chunks, depth, 16, width), bf16),
+            pltpu.VMEM((chunks, depth, 16, width), bf16),
+            pltpu.VMEM((chunks, depth, 16, width), bf16),
+            pltpu.VMEM((rows, chunks * 8, lanes), bf16),
             pltpu.VMEM((rows, kept, local, panel), bf16),
             pltpu.VMEM((rows, chunks, 8, lanes), f32),
             pltpu.VMEM((rows, chunks, 8, lanes), f32),
-            pltpu.VMEM((rows, chunks, 8, lanes), f32),
+            pltpu.VMEM((rows, chunks * 8, lanes), bf16),
             sem((2, chunks)),
             sem((2, rows - 1)),
             sem((2, rows - 1)),
@@ -409,8 +428,6 @@
             collective_id=0, has_side_effects=True, vmem_limit_bytes=63 * 1024 * 1024
         ),
     )(tail_factor, tail_solution, coupling, inverse_blocks, sources, station_map[None, :])
-    used = gathered[..., : panels * 2 * local].reshape(rows, chunks, 8, panels, 2, local)
-    return jnp.transpose(used, (3, 4, 5, 1, 0, 2)).reshape(panels, 2, local, rhs)
 
 
 def plan(mesh):
@@ -423,7 +440,7 @@
             and rows >= 8
             and tail_factor.shape[2] % 128 == 0
             and (rows * 8) % 128 == 0
-            and tail_solution.shape[2] % (rows * 8) == 0
+            and tail_solution.shape[2] % (rows * 16) == 0
             and inverse_blocks.shape[2] % 16 == 0
             and inverse_blocks.shape[3] % 128 == 0
         )

time: 53.9 us -> 50.5 us (0.937)
  Pallas kernels: 51.3 us -> 48.8 us
  local copies, waits for them, and re-layouts: 2.38 us -> 1.54 us
    pallas_call x1, Pallas kernels: 51.3 us -> 48.8 us  [fused_shards(): pl.pallas_call(functools.partial(fused_kernel, rows, depth, panels, chunk...]
    reshape x3 -> x0, local copies, waits for them, and re-layouts: 2.38 us -> none  [the longest x2 1.5 us: fused_shards(): gathered[..., :panels * 2 * local]]
    unnamed x0 -> x1, local copies, waits for them, and re-layouts: none -> 1.54 us
where the time goes in v3:
time: 50.5 us; the launch traced here: 50.4 us
  Pallas kernels  48.8 us (97%)
  local copies, waits for them, and re-layouts  1.54 us (3%)
    pallas_call x1, Pallas kernels, fused_shards(): pl.pallas_call(functools.partial(fused_kernel, rows, depth, panels, chunk...  48.8 us
    unnamed x1, local copies, waits for them, and re-layouts  1.54 us

profile of v3, /device:TPU:0, one launch (start us, length us, event | category | flops | bytes accessed | tf_op | source)
XLA Modules:
  0.0 50.4 jit_solution(7051751353268630213)
XLA Ops:
  0.0 48.8 %shard_map.64 = f32[3,2,16,256]{3,2,1,0:T(8,128)} custom-call(bf16[2,1024,384]{2,1,0:T(8,128)(2,1)} %factor_h.1, bf16[2,1024,256]{2,1,0:T(8,128)(2,1)} %tail_h.1, bf16[3,2,16,768]{3,2,1,0:T(8,128)(2,1)} %coupling_h.1, f32[3,2,16,256]{3,2,1,0:T(8,128)} %inverse_h.1, f32[3,2,16,512]{3,2,1,0:T(8,128)} %sources_h.1, s32[1,256]{1,0:T(1,128)} %bitcast.1), custom_call_target="tpu_custom_call" | custom-call | tf_op jit(solution)/shard_map/pallas_call | solution.py:386
  48.8 1.5 %copy.8 = f32[3,2,16,256]{3,2,1,0:T(8,128)} copy(f32[3,2,16,256]{3,2,1,0:T(8,128)} %shard_map.64) | data formatting | bytes 196608

commit v4 on v3

--- a/solution.py
+++ b/solution.py
@@ -353,7 +353,7 @@
     filler = [jnp.zeros((count_r, lanes - kinds * local), jnp.float32)] if lanes > kinds * local else []
     for r in range(rows):
         pieces = [value[:, r * local:(r + 1) * local] for value in solved] + filler
-        sol_out[r] = jnp.concatenate(pieces, axis=1).astype(jnp.bfloat16)
+        sol_out[r] = jnp.concatenate(pieces, axis=1)
     sol_copies = [
         send(sol_out.at[peer], sol_in.at[my_slot], sol_s, peer, col, d)
         for d, peer in enumerate(peers)
@@ -361,7 +361,7 @@
     sol_in[my_slot] = sol_out[row]
     for copy in sol_copies:
         copy.wait_recv()
-    found = sol_in[...].astype(jnp.float32)
+    found = sol_in[...]
     for q in range(chunks):
         turned = jnp.transpose(found[:, q * 8:(q + 1) * 8].reshape(span, lanes))
         out[:, :, :, q * span:(q + 1) * span] = turned[:kinds * local].reshape(
@@ -407,11 +407,11 @@
             pltpu.VMEM((chunks, depth, 16, width), bf16),
             pltpu.VMEM((chunks, depth, 16, width), bf16),
             pltpu.VMEM((chunks, depth, 16, width), bf16),
-            pltpu.VMEM((rows, chunks * 8, lanes), bf16),
+            pltpu.VMEM((rows, chunks * 8, lanes), f32),
             pltpu.VMEM((rows, kept, local, panel), bf16),
             pltpu.VMEM((rows, chunks, 8, lanes), f32),
             pltpu.VMEM((rows, chunks, 8, lanes), f32),
-            pltpu.VMEM((rows, chunks * 8, lanes), bf16),
+            pltpu.VMEM((rows, chunks * 8, lanes), f32),
             sem((2, chunks)),
             sem((2, rows - 1)),
             sem((2, rows - 1)),

time: 50.5 us -> 50.7 us (level)
  no operation moved by 1% of the time
where the time goes in v4:
time: 50.7 us; the launch traced here: 50.6 us
  Pallas kernels  49 us (97%)
  local copies, waits for them, and re-layouts  1.54 us (3%)
    pallas_call x1, Pallas kernels, fused_shards(): pl.pallas_call(functools.partial(fused_kernel, rows, depth, panels, chunk...  49 us
    unnamed x1, local copies, waits for them, and re-layouts  1.54 us

profile of v4, /device:TPU:0, one launch (start us, length us, event | category | flops | bytes accessed | tf_op | source)
XLA Modules:
  0.0 50.6 jit_solution(10919467582040104278)
XLA Ops:
  0.0 49.0 %shard_map.64 = f32[3,2,16,256]{3,2,1,0:T(8,128)} custom-call(bf16[2,1024,384]{2,1,0:T(8,128)(2,1)} %factor_h.1, bf16[2,1024,256]{2,1,0:T(8,128)(2,1)} %tail_h.1, bf16[3,2,16,768]{3,2,1,0:T(8,128)(2,1)} %coupling_h.1, f32[3,2,16,256]{3,2,1,0:T(8,128)} %inverse_h.1, f32[3,2,16,512]{3,2,1,0:T(8,128)} %sources_h.1, s32[1,256]{1,0:T(1,128)} %bitcast.1), custom_call_target="tpu_custom_call" | custom-call | tf_op jit(solution)/shard_map/pallas_call | solution.py:386
  49.0 1.5 %copy.8 = f32[3,2,16,256]{3,2,1,0:T(8,128)} copy(f32[3,2,16,256]{3,2,1,0:T(8,128)} %shard_map.64) | data formatting | bytes 196608
